TPU v7x, 256 devices: a whole 4x4x8 slice. The times are simulated.
256 devices in a mesh: depth: 16 (over z, core), image: 16 (over x, y).
Axes of the slice: x: 4, y: 4, z: 8, core: 2. Of those that a mesh axis runs over, the one named last changes fastest.
Arguments:
- level_set: float32 [256, 1024, 512], P('depth', 'image'), may hold values from -6 to 6
- velocity: float32 [3, 256, 1024, 512], P(None, 'depth', 'image'), may hold values from -1 to 1
- view_flag: int32 [16], replicated, may hold values from 0 to 1
- slab_rank: int32 [16], replicated, may hold values from 0 to 15, each once
Outputs:
- image_first: float32 [4, 1024, 512], P(None, 'image', 'depth')
- image_second: float32 [4, 1024, 512], P(None, 'image', 'depth')
- level_next: float32 [256, 1024, 512], P('depth', 'image')
Inputs may be any that keep to these rules, and one draw needn't show every extreme that they name: `slab_rank`: each of 0 to 15 once.
All inputs are finite; a program needn't handle non-finite values.
Results may differ from a plain program's by a relative error of at most 0.00013.
Values sent between devices are 32-bit elements; how exact they have to be, the bound alone decides.
A program may use at most 64 MiB of HBM per device.

v0:
```python
import jax
import jax.numpy as jnp
from jax import lax
from jax.sharding import PartitionSpec as P

STEPS = 4
step_size = 0.3


def padded_2(array, sides, width):
    edges = {}
    for axis, dim in sides:
        size, length = (lax.axis_size(axis), array.shape[dim])
        up = [(i, (i + 1) % size) for i in range(size - 1)]
        last = lax.slice_in_dim(array, length - width, length, axis=dim)
        leading = lax.slice_in_dim(array, 0, width, axis=dim)
        edges[dim] = (
            lax.ppermute(last, axis, up),
            lax.ppermute(leading, axis, [(b, a) for a, b in up]),
        )
    done = []
    for _, dim in sides:
        low, high = edges[dim]
        around = [(width, width) if d in done else (0, 0) for d in range(array.ndim)]
        array = jnp.concatenate([jnp.pad(low, around), array, jnp.pad(high, around)], axis=dim)
        done.append(dim)
    return array


def update(padded, velocity):
    center = padded[1:-1, 1:-1, 1:-1]
    lows = (padded[:-2, 1:-1, 1:-1], padded[1:-1, :-2, 1:-1], padded[1:-1, 1:-1, :-2])
    highs = (padded[2:, 1:-1, 1:-1], padded[1:-1, 2:, 1:-1], padded[1:-1, 1:-1, 2:])
    rate = jnp.zeros_like(center)
    for k in range(3):
        speed = velocity[k]
        rate = (
            rate
            + jnp.maximum(speed, 0.0) * (center - lows[k])
            + jnp.minimum(speed, 0.0) * (highs[k] - center)
        )
    return center - step_size * rate


def advect_single(field, velocity):
    padded = padded_2(field, (("depth", 0), ("image", 1)), 1)
    padded = jnp.pad(padded, ((0, 0), (0, 0), (1, 1)))
    return update(padded, velocity)


def render_brick(field, flag, scale):
    density = scale * jnp.exp(-field * field)
    colour = jnp.stack(
        [jax.nn.sigmoid(2.0 * field), jnp.exp(-field * field), jax.nn.sigmoid(-2.0 * field)], axis=0
    )
    running = jnp.cumsum(density, axis=0)
    totals = running[-1:]
    before = jnp.where(flag[0] == 0, running - density, totals - running)
    weight = jnp.exp(-before) * (1.0 - jnp.exp(-density))
    partial_colour = jnp.sum(weight[None] * colour, axis=1)
    return (partial_colour, -totals[0])


def composite(frames, slab_rank):
    count = len(frames)
    depth_count = lax.axis_size("depth")
    colours = jnp.stack([frame[0] for frame in frames], axis=0)
    logs = jnp.stack([frame[1] for frame in frames], axis=0)
    rows, cols = (logs.shape[1], logs.shape[2])
    width = cols // depth_count
    packed = jnp.concatenate([colours, logs[:, None]], axis=1)
    received = lax.all_to_all(packed, "depth", split_axis=3, concat_axis=0, tiled=True)
    received = received.reshape(depth_count, count, 4, rows, width)
    earlier_mask = (slab_rank[None, :] < slab_rank[:, None]).astype(jnp.float32)
    log_parts = received[:, :, 3]
    earlier = jnp.einsum("de,efxy->dfxy", earlier_mask, log_parts, precision=lax.Precision.HIGHEST)
    rgb = jnp.sum(jnp.exp(earlier)[:, :, None] * received[:, :, :3], axis=0)
    alpha = 1.0 - jnp.exp(jnp.sum(log_parts, axis=0))
    result = jnp.concatenate([rgb, alpha[:, None]], axis=1)
    return [result[0]]


def local(level_set, velocity, view_flag, slab_rank):
    scale = 2.0 / (level_set.shape[0] * lax.axis_size("depth"))
    own_flag = lax.dynamic_slice_in_dim(view_flag, lax.axis_index("depth"), 1)
    first = render_brick(level_set, own_flag, scale)
    field = level_set
    for step in range(STEPS):
        field = advect_single(field, velocity)
    second = render_brick(field, own_flag, scale)
    image_first = composite([first], slab_rank)[0]
    image_second = composite([second], slab_rank)[0]
    return (image_first, image_second, field)


def solution(mesh):
    placed = (P("depth", "image", None), P(None, "depth", "image", None), P(), P())
    return jax.shard_map(
        local,
        mesh=mesh,
        in_specs=placed,
        out_specs=(P(None, "image", "depth"), P(None, "image", "depth"), P("depth", "image", None)),
        check_vma=False,
    )
```

profile of v0, /device:TPU:27, one launch (start us, length us, event | category | flops | bytes accessed | tf_op | source)
XLA Modules:
  0.0 151.2 jit_solution(3199686916753563401)
XLA Ops:
  1.7 2.4 %collective-permute-start.3 = (f32[16,1,512]{2,1,0:T(1,128)S(1)}, f32[16,1,512]{2,1,0:T(1,128)S(1)}, u32[]{:S(2)}, u32[]{:S(2)}) collective-permute-start(f32[16,1,512]{2,1,0:T(1,128)S(1)} %get-tuple-element.28), channel_id=1, source_target_pairs={{1,0},{2,1},{3,2},{4,3},{5,4},{6,5},{7,6},{8,7},{9,8},{10,9},{11,1... | collective-permute-start | bytes 98312 | tf_op jit(solution)/shard_map/ppermute | solution.py:19
  5.1 4.4 %collective-permute-start = (f32[1,64,512]{2,1,0:T(8,128)S(1)}, f32[1,64,512]{2,1,0:T(8,128)S(1)}, u32[]{:S(2)}, u32[]{:S(2)}) collective-permute-start(f32[1,64,512]{2,1,0:T(8,128)S(1)} %get-tuple-element.30), channel_id=1, source_target_pairs={{0,16},{16,32},{32,48},{48,64},{64,80},{80,96},{96,112},{112,128},... | collective-permute-start | bytes 393224 | tf_op jit(solution)/shard_map/ppermute | solution.py:18
  9.5 1.9 %collective-permute-start.1 = (f32[1,64,512]{2,1,0:T(8,128)S(1)}, f32[1,64,512]{2,1,0:T(8,128)S(1)}, u32[]{:S(2)}, u32[]{:S(2)}) collective-permute-start(f32[1,64,512]{2,1,0:T(8,128)S(1)} %get-tuple-element.29), channel_id=1, source_target_pairs={{16,0},{32,16},{48,32},{64,48},{80,64},{96,80},{112,96},{128,112},... | collective-permute-start | bytes 393224 | tf_op jit(solution)/shard_map/ppermute | solution.py:19
  11.4 5.0 %collective-permute-start.2 = (f32[16,1,512]{2,1,0:T(1,128)S(1)}, f32[16,1,512]{2,1,0:T(1,128)S(1)}, u32[]{:S(2)}, u32[]{:S(2)}) collective-permute-start(f32[16,1,512]{2,1,0:T(1,128)S(1)} %get-tuple-element.27), channel_id=1, source_target_pairs={{0,1},{1,2},{2,3},{3,4},{4,5},{5,6},{6,7},{7,8},{8,9},{9,10},{10,1... | collective-permute-start | bytes 98312 | tf_op jit(solution)/shard_map/ppermute | solution.py:18
  16.5 2.2 %fusion.75 = f32[16,64,512]{2,1,0:T(8,128)S(1)} fusion(f32[16,64,512]{2,1,0:T(8,128)} %param.4), kind=kOutput, calls=%fused_computation.143 | output fusion | flops 9437184 | bytes 4194304 | tf_op jit(solution)/shard_map/jit(cumsum)/reduce_window_sum | solution.py:56
  25.7 6.7 %fusion.59 = (f32[16,64,512]{2,1,0:T(8,128)S(1)}, f32[1,16,64,512]{3,2,1,0:T(8,128)}, f32[16,64,512]{2,1,0:T(8,128)}, f32[1,16,64,512]{3,2,1,0:T(8,128)}, f32[1,16,64,512]{3,2,1,0:T(8,128)}) fusion(f32[16,64,512]{2,1,0:T(8,128)S(1)} %copy-done, f32[18,66,514]{2,1,0:T(8,128)S(1)} %select_maximum_fusion.12, f32[18,1,512]{2,1,0:T(1,128)S(1)} %pad.39, ...), kind=kLoop, calls=%fused_computation.110 | loop fusion | flops 24641536 | bytes 27992064 | tf_op jit(solution)/shard_map/sub | solution.py:42
  32.4 1.9 %collective-permute-start.5 = (f32[1,64,512]{2,1,0:T(8,128)S(1)}, f32[1,64,512]{2,1,0:T(8,128)S(1)}, u32[]{:S(2)}, u32[]{:S(2)}) collective-permute-start(f32[1,64,512]{2,1,0:T(8,128)S(1)} %get-tuple-element.19), channel_id=1, source_target_pairs={{16,0},{32,16},{48,32},{64,48},{80,64},{96,80},{112,96},{128,112},... | collective-permute-start | bytes 393224 | tf_op jit(solution)/shard_map/ppermute | solution.py:19
  34.4 3.9 %collective-permute-start.4 = (f32[1,64,512]{2,1,0:T(8,128)S(1)}, f32[1,64,512]{2,1,0:T(8,128)S(1)}, u32[]{:S(2)}, u32[]{:S(2)}) collective-permute-start(f32[1,64,512]{2,1,0:T(8,128)S(1)} %get-tuple-element.18), channel_id=1, source_target_pairs={{0,16},{16,32},{32,48},{48,64},{64,80},{80,96},{96,112},{112,128},... | collective-permute-start | bytes 393224 | tf_op jit(solution)/shard_map/ppermute | solution.py:18
  40.3 5.5 %collective-permute-start.6 = (f32[16,1,512]{2,1,0:T(1,128)S(1)}, f32[16,1,512]{2,1,0:T(1,128)S(1)}, u32[]{:S(2)}, u32[]{:S(2)}) collective-permute-start(f32[16,1,512]{2,1,0:T(1,128)S(1)} %get-tuple-element.20), channel_id=1, source_target_pairs={{0,1},{1,2},{2,3},{3,4},{4,5},{5,6},{6,7},{7,8},{8,9},{9,10},{10,1... | collective-permute-start | bytes 98312 | tf_op jit(solution)/shard_map/ppermute | solution.py:18
  46.8 3.0 %select_maximum_fusion.8 = f32[18,66,514]{2,1,0:T(8,128)S(1)} fusion(f32[18,1,512]{2,1,0:T(1,128)S(1)} %pad.42, f32[18,1,512]{2,1,0:T(1,128)S(1)} %pad.41, f32[1,64,512]{2,1,0:T(8,128)S(1)} %collective-permute-done.5, f32[16,64,512]{2,1,0:T(8,128)S(1)} %get-tuple-element.22, f32[1,64,512]{2,1,0:T(8,128)S(1)} %collective-permute-done.4), kind=kLoop, calls=%fused_computation.14 | loop fusion | flops 7327584 | bytes 4875552 | tf_op jit(solution)/shard_map/concatenate | solution.py:25
  49.9 3.5 %fusion.42 = f32[16,64,512]{2,1,0:T(8,128)S(1)} fusion(f32[16,64,512]{2,1,0:T(8,128)S(1)} %get-tuple-element.22, f32[18,66,514]{2,1,0:T(8,128)S(1)} %select_maximum_fusion.8, f32[18,1,512]{2,1,0:T(1,128)S(1)} %pad.42, f32[1,64,512]{2,1,0:T(8,128)S(1)} %collective-permute-done.5, f32[1,64,512]{2,1,0:T(8,128)S(1)} %collective-permute-done.4, ...), kind=kLoop, calls=%fused_computation.83 | loop fusion | flops 17301504 | bytes 15015936 | tf_op jit(solution)/shard_map/sub | solution.py:42
  53.5 1.9 %collective-permute-start.11 = (f32[16,1,512]{2,1,0:T(1,128)S(1)}, f32[16,1,512]{2,1,0:T(1,128)S(1)}, u32[]{:S(2)}, u32[]{:S(2)}) collective-permute-start(f32[16,1,512]{2,1,0:T(1,128)S(1)} %get-tuple-element.17), channel_id=1, source_target_pairs={{1,0},{2,1},{3,2},{4,3},{5,4},{6,5},{7,6},{8,7},{9,8},{10,9},{11,1... | collective-permute-start | bytes 98312 | tf_op jit(solution)/shard_map/ppermute | solution.py:19
  55.4 5.8 %collective-permute-start.10 = (f32[16,1,512]{2,1,0:T(1,128)S(1)}, f32[16,1,512]{2,1,0:T(1,128)S(1)}, u32[]{:S(2)}, u32[]{:S(2)}) collective-permute-start(f32[16,1,512]{2,1,0:T(1,128)S(1)} %get-tuple-element.16), channel_id=1, source_target_pairs={{0,1},{1,2},{2,3},{3,4},{4,5},{5,6},{6,7},{7,8},{8,9},{9,10},{10,1... | collective-permute-start | bytes 98312 | tf_op jit(solution)/shard_map/ppermute | solution.py:18
  61.1 2.1 %collective-permute-start.9 = (f32[1,64,512]{2,1,0:T(8,128)S(1)}, f32[1,64,512]{2,1,0:T(8,128)S(1)}, u32[]{:S(2)}, u32[]{:S(2)}) collective-permute-start(f32[1,64,512]{2,1,0:T(8,128)S(1)} %get-tuple-element.15), channel_id=1, source_target_pairs={{16,0},{32,16},{48,32},{64,48},{80,64},{96,80},{112,96},{128,112},... | collective-permute-start | bytes 393224 | tf_op jit(solution)/shard_map/ppermute | solution.py:19
  63.3 4.2 %collective-permute-start.8 = (f32[1,64,512]{2,1,0:T(8,128)S(1)}, f32[1,64,512]{2,1,0:T(8,128)S(1)}, u32[]{:S(2)}, u32[]{:S(2)}) collective-permute-start(f32[1,64,512]{2,1,0:T(8,128)S(1)} %get-tuple-element.14), channel_id=1, source_target_pairs={{0,16},{16,32},{32,48},{48,64},{64,80},{80,96},{96,112},{112,128},... | collective-permute-start | bytes 393224 | tf_op jit(solution)/shard_map/ppermute | solution.py:18
  69.2 3.0 %select_maximum_fusion.4 = f32[18,66,514]{2,1,0:T(8,128)S(1)} fusion(f32[18,1,512]{2,1,0:T(1,128)S(1)} %pad.45, f32[18,1,512]{2,1,0:T(1,128)S(1)} %pad.44, f32[1,64,512]{2,1,0:T(8,128)S(1)} %collective-permute-done.9, f32[16,64,512]{2,1,0:T(8,128)S(1)} %fusion.42, f32[1,64,512]{2,1,0:T(8,128)S(1)} %collective-permute-done.8), kind=kLoop, calls=%fused_computation.10 | loop fusion | flops 7327584 | bytes 4875552 | tf_op jit(solution)/shard_map/concatenate | solution.py:25
  72.2 3.5 %fusion.25 = f32[16,64,512]{2,1,0:T(8,128)S(1)} fusion(f32[16,64,512]{2,1,0:T(8,128)S(1)} %fusion.42, f32[18,66,514]{2,1,0:T(8,128)S(1)} %select_maximum_fusion.4, f32[18,1,512]{2,1,0:T(1,128)S(1)} %pad.45, f32[1,64,512]{2,1,0:T(8,128)S(1)} %collective-permute-done.9, f32[1,64,512]{2,1,0:T(8,128)S(1)} %collective-permute-done.8, f32[18,1,512]{2,1,0:T(1,128)S(1)} %pad.44, ...), kind=kLoop, calls=%fused_computation.56 | loop fusion | flops 17301504 | bytes 15015936 | tf_op jit(solution)/shard_map/sub | solution.py:42
  78.3 4.4 %collective-permute-start.12 = (f32[1,64,512]{2,1,0:T(8,128)S(1)}, f32[1,64,512]{2,1,0:T(8,128)S(1)}, u32[]{:S(2)}, u32[]{:S(2)}) collective-permute-start(f32[1,64,512]{2,1,0:T(8,128)S(1)} %get-tuple-element.10), channel_id=1, source_target_pairs={{0,16},{16,32},{32,48},{48,64},{64,80},{80,96},{96,112},{112,128},... | collective-permute-start | bytes 393224 | tf_op jit(solution)/shard_map/ppermute | solution.py:18
  85.3 5.5 %collective-permute-start.14 = (f32[16,1,512]{2,1,0:T(1,128)}, f32[16,1,512]{2,1,0:T(1,128)}, u32[]{:S(2)}, u32[]{:S(2)}) collective-permute-start(f32[16,1,512]{2,1,0:T(1,128)} %get-tuple-element.12), channel_id=1, source_target_pairs={{0,1},{1,2},{2,3},{3,4},{4,5},{5,6},{6,7},{7,8},{8,9},{9,10},{10,1... | collective-permute-start | bytes 98312 | tf_op jit(solution)/shard_map/ppermute | solution.py:18
  95.0 11.1 %all-to-all-start = ((f32[16,1,8192]{2,1,0:T(1,128)}), f32[16,1,8192]{2,1,0:T(1,128)S(1)}, u32[]{:S(2)}, u32[]{:S(2)}) async-start(f32[16,1,8192]{2,1,0:T(1,128)} %reshape.111), calls=%async_computation | async-start | bytes 1048576 | tf_op jit(solution)/shard_map/all_to_all | solution.py:72
  107.7 3.0 %select_maximum_fusion = f32[18,66,514]{2,1,0:T(8,128)S(1)} fusion(f32[18,1,512]{2,1,0:T(1,128)S(1)} %pad.48, f32[18,1,512]{2,1,0:T(1,128)S(1)} %pad.47, f32[1,64,512]{2,1,0:T(8,128)S(1)} %collective-permute-done.13, f32[16,64,512]{2,1,0:T(8,128)S(1)} %copy-done.2, f32[1,64,512]{2,1,0:T(8,128)S(1)} %collective-permute-done.12), kind=kLoop, calls=%fused_computation.6 | loop fusion | flops 7327584 | bytes 4875552 | tf_op jit(solution)/shard_map/concatenate | solution.py:25
  110.7 5.5 %divide_bitcast_fusion.1 = (f32[1,16,64,512]{3,2,1,0:T(8,128)S(1)}, f32[16,64,512]{2,1,0:T(8,128)S(1)}) fusion(f32[16,64,512]{2,1,0:T(8,128)S(1)} %copy-done.2, f32[18,66,514]{2,1,0:T(8,128)S(1)} %select_maximum_fusion, f32[3,16,64,512]{3,2,1,0:T(8,128)} %param.5, f32[18,1,512]{2,1,0:T(1,128)S(1)} %pad.48, f32[1,64,512]{2,1,0:T(8,128)S(1)} %collective-permute-done.13, ...), kind=kLoop, calls=%fused_computation.130 | loop fusion | flops 19398656 | bytes 17113088 | tf_op jit(solution)/shard_map/stack | solution.py:53
  123.4 6.0 %all-to-all-start.1 = ((f32[16,1,8192]{2,1,0:T(1,128)}), f32[16,1,8192]{2,1,0:T(1,128)S(1)}, u32[]{:S(2)}, u32[]{:S(2)}) async-start(f32[16,1,8192]{2,1,0:T(1,128)} %reshape.113), calls=%async_computation.1 | async-start | bytes 1048576 | tf_op jit(solution)/shard_map/all_to_all | solution.py:72
  134.4 12.4 %all-to-all-done.1 = f32[16,1,8192]{2,1,0:T(1,128)S(1)} async-done(((f32[16,1,8192]{2,1,0:T(1,128)}), f32[16,1,8192]{2,1,0:T(1,128)S(1)}, u32[]{:S(2)}, u32[]{:S(2)}) %all-to-all-start.1) | async-done | bytes 524320 | tf_op jit(solution)/shard_map/all_to_all | solution.py:72
  (99 shorter events, 40.6 us)
Async XLA Ops:
  1.7 19.5 %collective-permute-start.3 = (f32[16,1,512]{2,1,0:T(1,128)S(1)}, f32[16,1,512]{2,1,0:T(1,128)S(1)}, u32[]{:S(2)}, u32[]{:S(2)}) collective-permute-start(f32[16,1,512]{2,1,0:T(1,128)S(1)} %get-tuple-element.28), channel_id=1, source_target_pairs={{1,0},{2,1},{3,2},{4,3},{5,4},{6,5},{7,6},{8,7},{9,8},{10,9},{11,1... | collective-permute-start | bytes 98312 | tf_op jit(solution)/shard_map/ppermute | solution.py:19
  5.1 16.2 %collective-permute-start = (f32[1,64,512]{2,1,0:T(8,128)S(1)}, f32[1,64,512]{2,1,0:T(8,128)S(1)}, u32[]{:S(2)}, u32[]{:S(2)}) collective-permute-start(f32[1,64,512]{2,1,0:T(8,128)S(1)} %get-tuple-element.30), channel_id=1, source_target_pairs={{0,16},{16,32},{32,48},{48,64},{64,80},{80,96},{96,112},{112,128},... | collective-permute-start | bytes 393224 | tf_op jit(solution)/shard_map/ppermute | solution.py:18
  9.5 13.8 %collective-permute-start.1 = (f32[1,64,512]{2,1,0:T(8,128)S(1)}, f32[1,64,512]{2,1,0:T(8,128)S(1)}, u32[]{:S(2)}, u32[]{:S(2)}) collective-permute-start(f32[1,64,512]{2,1,0:T(8,128)S(1)} %get-tuple-element.29), channel_id=1, source_target_pairs={{16,0},{32,16},{48,32},{64,48},{80,64},{96,80},{112,96},{128,112},... | collective-permute-start | bytes 393224 | tf_op jit(solution)/shard_map/ppermute | solution.py:19
  11.4 8.6 %copy-start.11 = (s32[16]{0:T(128)S(1)}, s32[16]{0:T(128)}, u32[]{:S(2)}) copy-start(s32[16]{0:T(128)} %param.6) | copy-start | bytes 196
  11.4 9.8 %collective-permute-start.2 = (f32[16,1,512]{2,1,0:T(1,128)S(1)}, f32[16,1,512]{2,1,0:T(1,128)S(1)}, u32[]{:S(2)}, u32[]{:S(2)}) collective-permute-start(f32[16,1,512]{2,1,0:T(1,128)S(1)} %get-tuple-element.27), channel_id=1, source_target_pairs={{0,1},{1,2},{2,3},{3,4},{4,5},{5,6},{6,7},{7,8},{8,9},{9,10},{10,1... | collective-permute-start | bytes 98312 | tf_op jit(solution)/shard_map/ppermute | solution.py:18
  32.4 14.4 %collective-permute-start.5 = (f32[1,64,512]{2,1,0:T(8,128)S(1)}, f32[1,64,512]{2,1,0:T(8,128)S(1)}, u32[]{:S(2)}, u32[]{:S(2)}) collective-permute-start(f32[1,64,512]{2,1,0:T(8,128)S(1)} %get-tuple-element.19), channel_id=1, source_target_pairs={{16,0},{32,16},{48,32},{64,48},{80,64},{96,80},{112,96},{128,112},... | collective-permute-start | bytes 393224 | tf_op jit(solution)/shard_map/ppermute | solution.py:19
  34.4 12.4 %collective-permute-start.4 = (f32[1,64,512]{2,1,0:T(8,128)S(1)}, f32[1,64,512]{2,1,0:T(8,128)S(1)}, u32[]{:S(2)}, u32[]{:S(2)}) collective-permute-start(f32[1,64,512]{2,1,0:T(8,128)S(1)} %get-tuple-element.18), channel_id=1, source_target_pairs={{0,16},{16,32},{32,48},{48,64},{64,80},{80,96},{96,112},{112,128},... | collective-permute-start | bytes 393224 | tf_op jit(solution)/shard_map/ppermute | solution.py:18
  38.4 7.4 %collective-permute-start.7 = (f32[16,1,512]{2,1,0:T(1,128)S(1)}, f32[16,1,512]{2,1,0:T(1,128)S(1)}, u32[]{:S(2)}, u32[]{:S(2)}) collective-permute-start(f32[16,1,512]{2,1,0:T(1,128)S(1)} %get-tuple-element.21), channel_id=1, source_target_pairs={{1,0},{2,1},{3,2},{4,3},{5,4},{6,5},{7,6},{8,7},{9,8},{10,9},{11,1... | collective-permute-start | bytes 98312 | tf_op jit(solution)/shard_map/ppermute | solution.py:19
  40.3 6.5 %collective-permute-start.6 = (f32[16,1,512]{2,1,0:T(1,128)S(1)}, f32[16,1,512]{2,1,0:T(1,128)S(1)}, u32[]{:S(2)}, u32[]{:S(2)}) collective-permute-start(f32[16,1,512]{2,1,0:T(1,128)S(1)} %get-tuple-element.20), channel_id=1, source_target_pairs={{0,1},{1,2},{2,3},{3,4},{4,5},{5,6},{6,7},{7,8},{8,9},{9,10},{10,1... | collective-permute-start | bytes 98312 | tf_op jit(solution)/shard_map/ppermute | solution.py:18
  49.8 17.6 %copy-start.6 = (f32[1,16,64,512]{3,2,1,0:T(8,128)S(1)}, f32[1,16,64,512]{3,2,1,0:T(8,128)}, u32[]{:S(2)}) copy-start(f32[1,16,64,512]{3,2,1,0:T(8,128)} %get-tuple-element.23) | copy-start | bytes 6291460
  49.8 17.6 %copy-start.7 = (f32[16,64,512]{2,1,0:T(8,128)S(1)}, f32[16,64,512]{2,1,0:T(8,128)}, u32[]{:S(2)}) copy-start(f32[16,64,512]{2,1,0:T(8,128)} %get-tuple-element.24) | copy-start | bytes 6291460
  49.8 17.6 %copy-start.8 = (f32[1,16,64,512]{3,2,1,0:T(8,128)S(1)}, f32[1,16,64,512]{3,2,1,0:T(8,128)}, u32[]{:S(2)}) copy-start(f32[1,16,64,512]{3,2,1,0:T(8,128)} %get-tuple-element.25) | copy-start | bytes 6291460
  49.9 17.6 %copy-start.9 = (f32[1,16,64,512]{3,2,1,0:T(8,128)S(1)}, f32[1,16,64,512]{3,2,1,0:T(8,128)}, u32[]{:S(2)}) copy-start(f32[1,16,64,512]{3,2,1,0:T(8,128)} %get-tuple-element.26) | copy-start | bytes 6291460
  53.5 15.1 %collective-permute-start.11 = (f32[16,1,512]{2,1,0:T(1,128)S(1)}, f32[16,1,512]{2,1,0:T(1,128)S(1)}, u32[]{:S(2)}, u32[]{:S(2)}) collective-permute-start(f32[16,1,512]{2,1,0:T(1,128)S(1)} %get-tuple-element.17), channel_id=1, source_target_pairs={{1,0},{2,1},{3,2},{4,3},{5,4},{6,5},{7,6},{8,7},{9,8},{10,9},{11,1... | collective-permute-start | bytes 98312 | tf_op jit(solution)/shard_map/ppermute | solution.py:19
  55.4 13.2 %collective-permute-start.10 = (f32[16,1,512]{2,1,0:T(1,128)S(1)}, f32[16,1,512]{2,1,0:T(1,128)S(1)}, u32[]{:S(2)}, u32[]{:S(2)}) collective-permute-start(f32[16,1,512]{2,1,0:T(1,128)S(1)} %get-tuple-element.16), channel_id=1, source_target_pairs={{0,1},{1,2},{2,3},{3,4},{4,5},{5,6},{6,7},{7,8},{8,9},{9,10},{10,1... | collective-permute-start | bytes 98312 | tf_op jit(solution)/shard_map/ppermute | solution.py:18
  61.1 7.5 %collective-permute-start.9 = (f32[1,64,512]{2,1,0:T(8,128)S(1)}, f32[1,64,512]{2,1,0:T(8,128)S(1)}, u32[]{:S(2)}, u32[]{:S(2)}) collective-permute-start(f32[1,64,512]{2,1,0:T(8,128)S(1)} %get-tuple-element.15), channel_id=1, source_target_pairs={{16,0},{32,16},{48,32},{64,48},{80,64},{96,80},{112,96},{128,112},... | collective-permute-start | bytes 393224 | tf_op jit(solution)/shard_map/ppermute | solution.py:19
  63.3 5.9 %collective-permute-start.8 = (f32[1,64,512]{2,1,0:T(8,128)S(1)}, f32[1,64,512]{2,1,0:T(8,128)S(1)}, u32[]{:S(2)}, u32[]{:S(2)}) collective-permute-start(f32[1,64,512]{2,1,0:T(8,128)S(1)} %get-tuple-element.14), channel_id=1, source_target_pairs={{0,16},{16,32},{32,48},{48,64},{64,80},{80,96},{96,112},{112,128},... | collective-permute-start | bytes 393224 | tf_op jit(solution)/shard_map/ppermute | solution.py:18
  76.4 31.3 %collective-permute-start.13 = (f32[1,64,512]{2,1,0:T(8,128)}, f32[1,64,512]{2,1,0:T(8,128)S(1)}, u32[]{:S(2)}, u32[]{:S(2)}) collective-permute-start(f32[1,64,512]{2,1,0:T(8,128)} %get-tuple-element.11), channel_id=1, source_target_pairs={{16,0},{32,16},{48,32},{64,48},{80,64},{96,80},{112,96},{128,112},... | collective-permute-start | bytes 393224 | tf_op jit(solution)/shard_map/ppermute | solution.py:19
  78.3 29.4 %collective-permute-start.12 = (f32[1,64,512]{2,1,0:T(8,128)S(1)}, f32[1,64,512]{2,1,0:T(8,128)S(1)}, u32[]{:S(2)}, u32[]{:S(2)}) collective-permute-start(f32[1,64,512]{2,1,0:T(8,128)S(1)} %get-tuple-element.10), channel_id=1, source_target_pairs={{0,16},{16,32},{32,48},{48,64},{64,80},{80,96},{96,112},{112,128},... | collective-permute-start | bytes 393224 | tf_op jit(solution)/shard_map/ppermute | solution.py:18
  83.4 22.7 %collective-permute-start.15 = (f32[16,1,512]{2,1,0:T(1,128)}, f32[16,1,512]{2,1,0:T(1,128)}, u32[]{:S(2)}, u32[]{:S(2)}) collective-permute-start(f32[16,1,512]{2,1,0:T(1,128)} %get-tuple-element.13), channel_id=1, source_target_pairs={{1,0},{2,1},{3,2},{4,3},{5,4},{6,5},{7,6},{8,7},{9,8},{10,9},{11,1... | collective-permute-start | bytes 98312 | tf_op jit(solution)/shard_map/ppermute | solution.py:19
  85.3 21.6 %collective-permute-start.14 = (f32[16,1,512]{2,1,0:T(1,128)}, f32[16,1,512]{2,1,0:T(1,128)}, u32[]{:S(2)}, u32[]{:S(2)}) collective-permute-start(f32[16,1,512]{2,1,0:T(1,128)} %get-tuple-element.12), channel_id=1, source_target_pairs={{0,1},{1,2},{2,3},{3,4},{4,5},{5,6},{6,7},{7,8},{8,9},{9,10},{10,1... | collective-permute-start | bytes 98312 | tf_op jit(solution)/shard_map/ppermute | solution.py:18
  91.6 16.1 %copy-start.2 = (f32[16,64,512]{2,1,0:T(8,128)S(1)}, f32[16,64,512]{2,1,0:T(8,128)}, u32[]{:S(2)}) copy-start(f32[16,64,512]{2,1,0:T(8,128)} %copy-done.1) | copy-start | bytes 6291460
  95.0 28.4 %all-to-all-start = ((f32[16,1,8192]{2,1,0:T(1,128)}), f32[16,1,8192]{2,1,0:T(1,128)S(1)}, u32[]{:S(2)}, u32[]{:S(2)}) async-start(f32[16,1,8192]{2,1,0:T(1,128)} %reshape.111), calls=%async_computation | async-start | bytes 1048576 | tf_op jit(solution)/shard_map/all_to_all | solution.py:72
  123.4 23.4 %all-to-all-start.1 = ((f32[16,1,8192]{2,1,0:T(1,128)}), f32[16,1,8192]{2,1,0:T(1,128)S(1)}, u32[]{:S(2)}, u32[]{:S(2)}) async-start(f32[16,1,8192]{2,1,0:T(1,128)} %reshape.113), calls=%async_computation.1 | async-start | bytes 1048576 | tf_op jit(solution)/shard_map/all_to_all | solution.py:72
  (8 other events, 26.8 us)
where the time goes:
time: 152 us; the launch traced here: 151 us
  starting transfers between devices  71.7 us (47%)
  other arithmetic  42.2 us (28%)
  local copies, waits for them, and re-layouts  19.6 us (13%)
  waiting for transfers between devices  15.1 us (10%)
  between operations  2.04 us (1%)
    ppermute x8, starting transfers between devices, padded_2(): lax.ppermute(last, axis, up)  38.6 us
    all_to_all x2, starting transfers between devices, composite(): lax.all_to_all(packed, 'depth', split_axis=3, concat_axis=0, tiled=True)  17.1 us
    ppermute x8, starting transfers between devices, padded_2(): lax.ppermute(leading, axis, [(b, a) for a, b in up])  16 us
    sub x3, other arithmetic, update(): return center - step_size * rate  13.7 us
    all_to_all x2, waiting for transfers between devices, composite(): lax.all_to_all(packed, 'depth', split_axis=3, concat_axis=0, tiled=True)  13.6 us
    concatenate x4, other arithmetic, padded_2(): jnp.concatenate([jnp.pad(low, around), array, jnp.pad(high, around)], axi...  10.3 us
    unnamed x34, local copies, waits for them, and re-layouts  9.96 us
    another operation x1, other arithmetic, render_brick(): jnp.stack([jax.nn.sigmoid(2.0 * field), jnp.exp(-field * field), jax.nn.s...  5.46 us
  transfers between devices with their start and end apart: 18, of which 4 were waited for; matrix products, arithmetic and copies ran while one was open for 21% of the time, Pallas kernels for 0%

commit v1 on v0

--- a/solution.py
+++ b/solution.py
@@ -69,7 +69,10 @@
     rows, cols = (logs.shape[1], logs.shape[2])
     width = cols // depth_count
     packed = jnp.concatenate([colours, logs[:, None]], axis=1)
-    received = lax.all_to_all(packed, "depth", split_axis=3, concat_axis=0, tiled=True)
+    devices = lax.axis_size("depth")
+    blocks = jnp.stack(jnp.split(packed, devices, axis=3), axis=0)
+    blocks = lax.all_to_all(blocks, "depth", split_axis=0, concat_axis=0)
+    received = jnp.concatenate(blocks, axis=0)
     received = received.reshape(depth_count, count, 4, rows, width)
     earlier_mask = (slab_rank[None, :] < slab_rank[:, None]).astype(jnp.float32)
     log_parts = received[:, :, 3]

time: 152 us -> 171 us (1.12)
  other arithmetic: 42.2 us -> 57.9 us
  waiting for transfers between devices: 15.1 us -> 20 us
  starting transfers between devices: 71.7 us -> 69.9 us
    unnamed x1 -> x31, other arithmetic: 0.01 us -> 12.1 us
    ppermute x8, starting transfers between devices: 38.6 us -> 29.6 us  [padded_2(): lax.ppermute(last, axis, up)]
    ppermute x8, waiting for transfers between devices: 0.02 us -> 6.48 us  [padded_2(): lax.ppermute(leading, axis, [(b, a) for a, b in up])]
    all_to_all x2, starting transfers between devices: 17.1 us -> 21.2 us  [composite(): blocks = lax.all_to_all(blocks, 'depth', split_axis=0, concat_axis=0)]
    ppermute x8, starting transfers between devices: 16 us -> 19 us  [padded_2(): lax.ppermute(leading, axis, [(b, a) for a, b in up])]
    reduce_sum x2, other arithmetic: 2.17 us -> 5.06 us  [render_brick(): partial_colour = jnp.sum(weight[None] * colour, axis=1)]
    another operation x0 -> x2, local copies, waits for them, and re-layouts: none -> 2.77 us  [composite(): blocks = jnp.stack(jnp.split(packed, devices, axis=3), axis=0)]
    concatenate x2 -> x0, local copies, waits for them, and re-layouts: 1.97 us -> none  [composite(): packed = jnp.concatenate([colours, logs[:, None]], axis=1)]
  transfers between devices with their start and end apart: 18 -> 18, of which waited for: 4 -> 4; matrix products, arithmetic and copies ran while one was open for 21% -> 20% of each run, Pallas kernels for 0% -> 0%
where the time goes in v1:
time: 171 us; the launch traced here: 169 us
  starting transfers between devices  69.9 us (41%)
  other arithmetic  57.9 us (34%)
  waiting for transfers between devices  20 us (12%)
  local copies, waits for them, and re-layouts  18.3 us (11%)
  between operations  2.05 us (1%)
    ppermute x8, starting transfers between devices, padded_2(): lax.ppermute(last, axis, up)  29.6 us
    all_to_all x2, starting transfers between devices, composite(): blocks = lax.all_to_all(blocks, 'depth', split_axis=0, concat_axis=0)  21.2 us
    ppermute x8, starting transfers between devices, padded_2(): lax.ppermute(leading, axis, [(b, a) for a, b in up])  19 us
    sub x3, other arithmetic, update(): return center - step_size * rate  13.6 us
    all_to_all x2, waiting for transfers between devices, composite(): blocks = lax.all_to_all(blocks, 'depth', split_axis=0, concat_axis=0)  13.5 us
    unnamed x31, other arithmetic  12.1 us
    concatenate x4, other arithmetic, padded_2(): jnp.concatenate([jnp.pad(low, around), array, jnp.pad(high, around)], axi...  10.3 us
    unnamed x26, local copies, waits for them, and re-layouts  8.91 us
  transfers between devices with their start and end apart: 18, of which 4 were waited for; matrix products, arithmetic and copies ran while one was open for 20% of the time, Pallas kernels for 0%

profile of v1, /device:TPU:27, one launch (start us, length us, event | category | flops | bytes accessed | tf_op | source)
XLA Modules:
  0.0 169.0 jit_solution(9684758625917184334)
XLA Ops:
  1.6 4.1 %collective-permute-start = (f32[1,64,512]{2,1,0:T(8,128)S(1)}, f32[1,64,512]{2,1,0:T(8,128)S(1)}, u32[]{:S(2)}, u32[]{:S(2)}) collective-permute-start(f32[1,64,512]{2,1,0:T(8,128)S(1)} %get-tuple-element.30), channel_id=1, source_target_pairs={{0,16},{16,32},{32,48},{48,64},{64,80},{80,96},{96,112},{112,128},... | collective-permute-start | bytes 393224 | tf_op jit(solution)/shard_map/ppermute | solution.py:18
  8.8 2.8 %collective-permute-start.2 = (f32[16,1,512]{2,1,0:T(1,128)S(1)}, f32[16,1,512]{2,1,0:T(1,128)S(1)}, u32[]{:S(2)}, u32[]{:S(2)}) collective-permute-start(f32[16,1,512]{2,1,0:T(1,128)S(1)} %get-tuple-element.27), channel_id=1, source_target_pairs={{0,1},{1,2},{2,3},{3,4},{4,5},{5,6},{6,7},{7,8},{8,9},{9,10},{10,1... | collective-permute-start | bytes 98312 | tf_op jit(solution)/shard_map/ppermute | solution.py:18
  11.5 2.5 %collective-permute-start.3 = (f32[16,1,512]{2,1,0:T(1,128)S(1)}, f32[16,1,512]{2,1,0:T(1,128)S(1)}, u32[]{:S(2)}, u32[]{:S(2)}) collective-permute-start(f32[16,1,512]{2,1,0:T(1,128)S(1)} %get-tuple-element.28), channel_id=1, source_target_pairs={{1,0},{2,1},{3,2},{4,3},{5,4},{6,5},{7,6},{8,7},{9,8},{10,9},{11,1... | collective-permute-start | bytes 98312 | tf_op jit(solution)/shard_map/ppermute | solution.py:19
  23.4 6.7 %fusion.59 = (f32[16,64,512]{2,1,0:T(8,128)S(1)}, f32[1,16,64,512]{3,2,1,0:T(8,128)}, f32[16,64,512]{2,1,0:T(8,128)}, f32[1,16,64,512]{3,2,1,0:T(8,128)}, f32[1,16,64,512]{3,2,1,0:T(8,128)}) fusion(f32[16,64,512]{2,1,0:T(8,128)S(1)} %copy-done, f32[18,66,514]{2,1,0:T(8,128)S(1)} %select_maximum_fusion.12, f32[18,1,512]{2,1,0:T(1,128)S(1)} %pad.39, ...), kind=kLoop, calls=%fused_computation.140 | loop fusion | flops 24641536 | bytes 27992064 | tf_op jit(solution)/shard_map/sub | solution.py:42
  30.2 4.0 %fusion = f32[3,64,512]{2,1,0:T(8,128)S(1)} fusion(f32[1,16,64,512]{3,2,1,0:T(8,128)} %get-tuple-element.25, f32[1,16,64,512]{3,2,1,0:T(8,128)} %get-tuple-element.23, f32[1,16,64,512]{3,2,1,0:T(8,128)} %get-tuple-element.26, f32[16,64,512]{2,1,0:T(8,128)} %get-tuple-element.24), kind=kLoop, calls=%fused_computation.1 | loop fusion | flops 6193152 | bytes 8781824 | tf_op jit(solution)/shard_map/reduce_sum | solution.py:60
  43.0 4.5 %collective-permute-start.4 = (f32[1,64,512]{2,1,0:T(8,128)S(1)}, f32[1,64,512]{2,1,0:T(8,128)S(1)}, u32[]{:S(2)}, u32[]{:S(2)}) collective-permute-start(f32[1,64,512]{2,1,0:T(8,128)S(1)} %get-tuple-element.18), channel_id=1, source_target_pairs={{0,16},{16,32},{32,48},{48,64},{64,80},{80,96},{96,112},{112,128},... | collective-permute-start | bytes 393224 | tf_op jit(solution)/shard_map/ppermute | solution.py:18
  50.1 4.6 %collective-permute-start.6 = (f32[16,1,512]{2,1,0:T(1,128)S(1)}, f32[16,1,512]{2,1,0:T(1,128)S(1)}, u32[]{:S(2)}, u32[]{:S(2)}) collective-permute-start(f32[16,1,512]{2,1,0:T(1,128)S(1)} %get-tuple-element.20), channel_id=1, source_target_pairs={{0,1},{1,2},{2,3},{3,4},{4,5},{5,6},{6,7},{7,8},{8,9},{9,10},{10,1... | collective-permute-start | bytes 98312 | tf_op jit(solution)/shard_map/ppermute | solution.py:18
  57.4 4.0 %collective-permute-done.7 = f32[16,1,512]{2,1,0:T(1,128)S(1)} collective-permute-done((f32[16,1,512]{2,1,0:T(1,128)S(1)}, f32[16,1,512]{2,1,0:T(1,128)S(1)}, u32[]{:S(2)}, u32[]{:S(2)}) %collective-permute-start.7) | collective-permute-done | bytes 32800 | tf_op jit(solution)/shard_map/ppermute | solution.py:19
  61.5 3.0 %select_maximum_fusion.8 = f32[18,66,514]{2,1,0:T(8,128)S(1)} fusion(f32[18,1,512]{2,1,0:T(1,128)S(1)} %pad.42, f32[18,1,512]{2,1,0:T(1,128)S(1)} %pad.41, f32[1,64,512]{2,1,0:T(8,128)S(1)} %collective-permute-done.5, f32[16,64,512]{2,1,0:T(8,128)S(1)} %get-tuple-element.22, f32[1,64,512]{2,1,0:T(8,128)S(1)} %collective-permute-done.4), kind=kLoop, calls=%fused_computation.14 | loop fusion | flops 7327584 | bytes 4875552 | tf_op jit(solution)/shard_map/concatenate | solution.py:25
  64.5 3.4 %fusion.42 = f32[16,64,512]{2,1,0:T(8,128)S(1)} fusion(f32[16,64,512]{2,1,0:T(8,128)S(1)} %get-tuple-element.22, f32[18,66,514]{2,1,0:T(8,128)S(1)} %select_maximum_fusion.8, f32[18,1,512]{2,1,0:T(1,128)S(1)} %pad.42, f32[1,64,512]{2,1,0:T(8,128)S(1)} %collective-permute-done.5, f32[1,64,512]{2,1,0:T(8,128)S(1)} %collective-permute-done.4, ...), kind=kLoop, calls=%fused_computation.113 | loop fusion | flops 17301504 | bytes 15015936 | tf_op jit(solution)/shard_map/sub | solution.py:42
  67.9 5.1 %collective-permute-start.8 = (f32[1,64,512]{2,1,0:T(8,128)S(1)}, f32[1,64,512]{2,1,0:T(8,128)S(1)}, u32[]{:S(2)}, u32[]{:S(2)}) collective-permute-start(f32[1,64,512]{2,1,0:T(8,128)S(1)} %get-tuple-element.14), channel_id=1, source_target_pairs={{0,16},{16,32},{32,48},{48,64},{64,80},{80,96},{96,112},{112,128},... | collective-permute-start | bytes 393224 | tf_op jit(solution)/shard_map/ppermute | solution.py:18
  76.9 3.5 %collective-permute-start.11 = (f32[16,1,512]{2,1,0:T(1,128)S(1)}, f32[16,1,512]{2,1,0:T(1,128)S(1)}, u32[]{:S(2)}, u32[]{:S(2)}) collective-permute-start(f32[16,1,512]{2,1,0:T(1,128)S(1)} %get-tuple-element.17), channel_id=1, source_target_pairs={{1,0},{2,1},{3,2},{4,3},{5,4},{6,5},{7,6},{8,7},{9,8},{10,9},{11,1... | collective-permute-start | bytes 98312 | tf_op jit(solution)/shard_map/ppermute | solution.py:19
  81.2 2.4 %collective-permute-done.11 = f32[16,1,512]{2,1,0:T(1,128)S(1)} collective-permute-done((f32[16,1,512]{2,1,0:T(1,128)S(1)}, f32[16,1,512]{2,1,0:T(1,128)S(1)}, u32[]{:S(2)}, u32[]{:S(2)}) %collective-permute-start.11) | collective-permute-done | bytes 32800 | tf_op jit(solution)/shard_map/ppermute | solution.py:19
  83.7 3.0 %select_maximum_fusion.4 = f32[18,66,514]{2,1,0:T(8,128)S(1)} fusion(f32[18,1,512]{2,1,0:T(1,128)S(1)} %pad.45, f32[18,1,512]{2,1,0:T(1,128)S(1)} %pad.44, f32[1,64,512]{2,1,0:T(8,128)S(1)} %collective-permute-done.9, f32[16,64,512]{2,1,0:T(8,128)S(1)} %fusion.42, f32[1,64,512]{2,1,0:T(8,128)S(1)} %collective-permute-done.8), kind=kLoop, calls=%fused_computation.10 | loop fusion | flops 7327584 | bytes 4875552 | tf_op jit(solution)/shard_map/concatenate | solution.py:25
  86.7 3.5 %fusion.25 = f32[16,64,512]{2,1,0:T(8,128)S(1)} fusion(f32[16,64,512]{2,1,0:T(8,128)S(1)} %fusion.42, f32[18,66,514]{2,1,0:T(8,128)S(1)} %select_maximum_fusion.4, f32[18,1,512]{2,1,0:T(1,128)S(1)} %pad.45, f32[1,64,512]{2,1,0:T(8,128)S(1)} %collective-permute-done.9, f32[1,64,512]{2,1,0:T(8,128)S(1)} %collective-permute-done.8, f32[18,1,512]{2,1,0:T(1,128)S(1)} %pad.44, ...), kind=kLoop, calls=%fused_computation.86 | loop fusion | flops 17301504 | bytes 15015936 | tf_op jit(solution)/shard_map/sub | solution.py:42
  91.0 4.8 %collective-permute-start.12 = (f32[1,64,512]{2,1,0:T(8,128)}, f32[1,64,512]{2,1,0:T(8,128)S(1)}, u32[]{:S(2)}, u32[]{:S(2)}) collective-permute-start(f32[1,64,512]{2,1,0:T(8,128)} %get-tuple-element.10), channel_id=1, source_target_pairs={{0,16},{16,32},{32,48},{48,64},{64,80},{80,96},{96,112},{112,128},... | collective-permute-start | bytes 393224 | tf_op jit(solution)/shard_map/ppermute | solution.py:18
  100.3 3.4 %collective-permute-start.15 = (f32[16,1,512]{2,1,0:T(1,128)}, f32[16,1,512]{2,1,0:T(1,128)}, u32[]{:S(2)}, u32[]{:S(2)}) collective-permute-start(f32[16,1,512]{2,1,0:T(1,128)} %get-tuple-element.13), channel_id=1, source_target_pairs={{1,0},{2,1},{3,2},{4,3},{5,4},{6,5},{7,6},{8,7},{9,8},{10,9},{11,1... | collective-permute-start | bytes 98312 | tf_op jit(solution)/shard_map/ppermute | solution.py:19
  104.4 2.2 %copy.41 = f32[16,1,4,64,32]{3,4,2,1,0:T(8,128)S(1)} copy(f32[16,1,4,64,32]{4,3,2,1,0:T(8,128)} %fusion.178) | data formatting | bytes 1048576 | tf_op jit(solution)/shard_map/stack | solution.py:73
  108.1 14.1 %all-to-all-start = ((f32[16,1,8192]{2,1,0:T(1,128)}), f32[16,1,8192]{2,1,0:T(1,128)}, u32[]{:S(2)}, u32[]{:S(2)}) async-start(f32[16,1,8192]{2,1,0:T(1,128)} %reshape.107), calls=%async_computation | async-start | bytes 1048576 | tf_op jit(solution)/shard_map/all_to_all | solution.py:74
  123.8 3.0 %select_maximum_fusion = f32[18,66,514]{2,1,0:T(8,128)S(1)} fusion(f32[18,1,512]{2,1,0:T(1,128)S(1)} %pad.48, f32[18,1,512]{2,1,0:T(1,128)S(1)} %pad.47, f32[1,64,512]{2,1,0:T(8,128)S(1)} %collective-permute-done.13, f32[16,64,512]{2,1,0:T(8,128)S(1)} %copy-done.2, f32[1,64,512]{2,1,0:T(8,128)S(1)} %collective-permute-done.12), kind=kLoop, calls=%fused_computation.6 | loop fusion | flops 7327584 | bytes 4875552 | tf_op jit(solution)/shard_map/concatenate | solution.py:25
  126.8 5.5 %divide_bitcast_fusion.1 = (f32[1,16,64,512]{3,2,1,0:T(8,128)S(1)}, f32[16,64,512]{2,1,0:T(8,128)S(1)}) fusion(f32[16,64,512]{2,1,0:T(8,128)S(1)} %copy-done.2, f32[18,66,514]{2,1,0:T(8,128)S(1)} %select_maximum_fusion, f32[3,16,64,512]{3,2,1,0:T(8,128)} %param.5, f32[18,1,512]{2,1,0:T(1,128)S(1)} %pad.48, f32[1,64,512]{2,1,0:T(8,128)S(1)} %collective-permute-done.13, ...), kind=kLoop, calls=%fused_computation.160 | loop fusion | flops 19398656 | bytes 17113088 | tf_op jit(solution)/shard_map/stack | solution.py:53
  139.6 7.1 %all-to-all-start.1 = ((f32[16,1,8192]{2,1,0:T(1,128)}), f32[16,1,8192]{2,1,0:T(1,128)S(1)}, u32[]{:S(2)}, u32[]{:S(2)}) async-start(f32[16,1,8192]{2,1,0:T(1,128)} %reshape.109), calls=%async_computation.1 | async-start | bytes 1048576 | tf_op jit(solution)/shard_map/all_to_all | solution.py:74
  147.2 2.9 %reduce.7 = f32[16,8192]{1,0:T(8,128)S(1)} reduce(f32[16,1,8192]{2,1,0:T(1,128)} %all-to-all-done, f32[]{:T(128)} %broadcast.196), dimensions={1}, to_apply=%all_to_all.6.reduce_sub_computation | reduce | bytes 1048580 | tf_op jit(solution)/shard_map/all_to_all | solution.py:74
  150.6 13.4 %all-to-all-done.1 = f32[16,1,8192]{2,1,0:T(1,128)S(1)} async-done(((f32[16,1,8192]{2,1,0:T(1,128)}), f32[16,1,8192]{2,1,0:T(1,128)S(1)}, u32[]{:S(2)}, u32[]{:S(2)}) %all-to-all-start.1) | async-done | bytes 524320 | tf_op jit(solution)/shard_map/all_to_all | solution.py:74
  (120 shorter events, 53.5 us)
Async XLA Ops:
  1.6 17.3 %collective-permute-start = (f32[1,64,512]{2,1,0:T(8,128)S(1)}, f32[1,64,512]{2,1,0:T(8,128)S(1)}, u32[]{:S(2)}, u32[]{:S(2)}) collective-permute-start(f32[1,64,512]{2,1,0:T(8,128)S(1)} %get-tuple-element.30), channel_id=1, source_target_pairs={{0,16},{16,32},{32,48},{48,64},{64,80},{80,96},{96,112},{112,128},... | collective-permute-start | bytes 393224 | tf_op jit(solution)/shard_map/ppermute | solution.py:18
  5.7 15.2 %collective-permute-start.1 = (f32[1,64,512]{2,1,0:T(8,128)S(1)}, f32[1,64,512]{2,1,0:T(8,128)S(1)}, u32[]{:S(2)}, u32[]{:S(2)}) collective-permute-start(f32[1,64,512]{2,1,0:T(8,128)S(1)} %get-tuple-element.29), channel_id=1, source_target_pairs={{16,0},{32,16},{48,32},{64,48},{80,64},{96,80},{112,96},{128,112},... | collective-permute-start | bytes 393224 | tf_op jit(solution)/shard_map/ppermute | solution.py:19
  8.8 10.1 %collective-permute-start.2 = (f32[16,1,512]{2,1,0:T(1,128)S(1)}, f32[16,1,512]{2,1,0:T(1,128)S(1)}, u32[]{:S(2)}, u32[]{:S(2)}) collective-permute-start(f32[16,1,512]{2,1,0:T(1,128)S(1)} %get-tuple-element.27), channel_id=1, source_target_pairs={{0,1},{1,2},{2,3},{3,4},{4,5},{5,6},{6,7},{7,8},{8,9},{9,10},{10,1... | collective-permute-start | bytes 98312 | tf_op jit(solution)/shard_map/ppermute | solution.py:18
  11.5 6.0 %copy-start.7 = (s32[16]{0:T(128)S(1)}, s32[16]{0:T(128)}, u32[]{:S(2)}) copy-start(s32[16]{0:T(128)} %param.6) | copy-start | bytes 196
  11.5 7.3 %collective-permute-start.3 = (f32[16,1,512]{2,1,0:T(1,128)S(1)}, f32[16,1,512]{2,1,0:T(1,128)S(1)}, u32[]{:S(2)}, u32[]{:S(2)}) collective-permute-start(f32[16,1,512]{2,1,0:T(1,128)S(1)} %get-tuple-element.28), channel_id=1, source_target_pairs={{1,0},{2,1},{3,2},{4,3},{5,4},{6,5},{7,6},{8,7},{9,8},{10,9},{11,1... | collective-permute-start | bytes 98312 | tf_op jit(solution)/shard_map/ppermute | solution.py:19
  14.1 8.2 %slice-start = ((s8[6291456]{0:T(1024)(128)(4,1)}), s8[2097152]{0:T(1024)(128)(4,1)S(1)}, s32[]{:S(2)}) async-start(s8[6291456]{0:T(1024)(128)(4,1)} %bitcast.244), calls=%async_computation.2 | async-start | bytes 4194304
  18.9 3.4 %slice-start.1 = ((s8[6291456]{0:T(1024)(128)(4,1)}), s8[4194304]{0:T(1024)(128)(4,1)S(1)}, s32[]{:S(2)}) async-start(s8[6291456]{0:T(1024)(128)(4,1)} %bitcast.244), calls=%async_computation.3 | async-start | bytes 8388608
  43.0 18.5 %collective-permute-start.4 = (f32[1,64,512]{2,1,0:T(8,128)S(1)}, f32[1,64,512]{2,1,0:T(8,128)S(1)}, u32[]{:S(2)}, u32[]{:S(2)}) collective-permute-start(f32[1,64,512]{2,1,0:T(8,128)S(1)} %get-tuple-element.18), channel_id=1, source_target_pairs={{0,16},{16,32},{32,48},{48,64},{64,80},{80,96},{96,112},{112,128},... | collective-permute-start | bytes 393224 | tf_op jit(solution)/shard_map/ppermute | solution.py:18
  47.5 14.0 %collective-permute-start.5 = (f32[1,64,512]{2,1,0:T(8,128)S(1)}, f32[1,64,512]{2,1,0:T(8,128)S(1)}, u32[]{:S(2)}, u32[]{:S(2)}) collective-permute-start(f32[1,64,512]{2,1,0:T(8,128)S(1)} %get-tuple-element.19), channel_id=1, source_target_pairs={{16,0},{32,16},{48,32},{64,48},{80,64},{96,80},{112,96},{128,112},... | collective-permute-start | bytes 393224 | tf_op jit(solution)/shard_map/ppermute | solution.py:19
  50.1 7.3 %collective-permute-start.6 = (f32[16,1,512]{2,1,0:T(1,128)S(1)}, f32[16,1,512]{2,1,0:T(1,128)S(1)}, u32[]{:S(2)}, u32[]{:S(2)}) collective-permute-start(f32[16,1,512]{2,1,0:T(1,128)S(1)} %get-tuple-element.20), channel_id=1, source_target_pairs={{0,1},{1,2},{2,3},{3,4},{4,5},{5,6},{6,7},{7,8},{8,9},{9,10},{10,1... | collective-permute-start | bytes 98312 | tf_op jit(solution)/shard_map/ppermute | solution.py:18
  54.7 6.8 %collective-permute-start.7 = (f32[16,1,512]{2,1,0:T(1,128)S(1)}, f32[16,1,512]{2,1,0:T(1,128)S(1)}, u32[]{:S(2)}, u32[]{:S(2)}) collective-permute-start(f32[16,1,512]{2,1,0:T(1,128)S(1)} %get-tuple-element.21), channel_id=1, source_target_pairs={{1,0},{2,1},{3,2},{4,3},{5,4},{6,5},{7,6},{8,7},{9,8},{10,9},{11,1... | collective-permute-start | bytes 98312 | tf_op jit(solution)/shard_map/ppermute | solution.py:19
  67.9 15.8 %collective-permute-start.8 = (f32[1,64,512]{2,1,0:T(8,128)S(1)}, f32[1,64,512]{2,1,0:T(8,128)S(1)}, u32[]{:S(2)}, u32[]{:S(2)}) collective-permute-start(f32[1,64,512]{2,1,0:T(8,128)S(1)} %get-tuple-element.14), channel_id=1, source_target_pairs={{0,16},{16,32},{32,48},{48,64},{64,80},{80,96},{96,112},{112,128},... | collective-permute-start | bytes 393224 | tf_op jit(solution)/shard_map/ppermute | solution.py:18
  73.0 10.7 %collective-permute-start.9 = (f32[1,64,512]{2,1,0:T(8,128)S(1)}, f32[1,64,512]{2,1,0:T(8,128)S(1)}, u32[]{:S(2)}, u32[]{:S(2)}) collective-permute-start(f32[1,64,512]{2,1,0:T(8,128)S(1)} %get-tuple-element.15), channel_id=1, source_target_pairs={{16,0},{32,16},{48,32},{64,48},{80,64},{96,80},{112,96},{128,112},... | collective-permute-start | bytes 393224 | tf_op jit(solution)/shard_map/ppermute | solution.py:19
  74.9 6.3 %collective-permute-start.10 = (f32[16,1,512]{2,1,0:T(1,128)S(1)}, f32[16,1,512]{2,1,0:T(1,128)S(1)}, u32[]{:S(2)}, u32[]{:S(2)}) collective-permute-start(f32[16,1,512]{2,1,0:T(1,128)S(1)} %get-tuple-element.16), channel_id=1, source_target_pairs={{0,1},{1,2},{2,3},{3,4},{4,5},{5,6},{6,7},{7,8},{8,9},{9,10},{10,1... | collective-permute-start | bytes 98312 | tf_op jit(solution)/shard_map/ppermute | solution.py:18
  76.9 6.8 %collective-permute-start.11 = (f32[16,1,512]{2,1,0:T(1,128)S(1)}, f32[16,1,512]{2,1,0:T(1,128)S(1)}, u32[]{:S(2)}, u32[]{:S(2)}) collective-permute-start(f32[16,1,512]{2,1,0:T(1,128)S(1)} %get-tuple-element.17), channel_id=1, source_target_pairs={{1,0},{2,1},{3,2},{4,3},{5,4},{6,5},{7,6},{8,7},{9,8},{10,9},{11,1... | collective-permute-start | bytes 98312 | tf_op jit(solution)/shard_map/ppermute | solution.py:19
  90.2 7.5 %copy-start.1 = (f32[16,64,512]{2,1,0:T(8,128)}, f32[16,64,512]{2,1,0:T(8,128)S(1)}, u32[]{:S(2)}) copy-start(f32[16,64,512]{2,1,0:T(8,128)S(1)} %fusion.25) | copy-start | bytes 6291460
  91.0 32.8 %collective-permute-start.12 = (f32[1,64,512]{2,1,0:T(8,128)}, f32[1,64,512]{2,1,0:T(8,128)S(1)}, u32[]{:S(2)}, u32[]{:S(2)}) collective-permute-start(f32[1,64,512]{2,1,0:T(8,128)} %get-tuple-element.10), channel_id=1, source_target_pairs={{0,16},{16,32},{32,48},{48,64},{64,80},{80,96},{96,112},{112,128},... | collective-permute-start | bytes 393224 | tf_op jit(solution)/shard_map/ppermute | solution.py:18
  95.7 28.0 %collective-permute-start.13 = (f32[1,64,512]{2,1,0:T(8,128)S(1)}, f32[1,64,512]{2,1,0:T(8,128)S(1)}, u32[]{:S(2)}, u32[]{:S(2)}) collective-permute-start(f32[1,64,512]{2,1,0:T(8,128)S(1)} %get-tuple-element.11), channel_id=1, source_target_pairs={{16,0},{32,16},{48,32},{64,48},{80,64},{96,80},{112,96},{128,112},... | collective-permute-start | bytes 393224 | tf_op jit(solution)/shard_map/ppermute | solution.py:19
  98.4 23.8 %collective-permute-start.14 = (f32[16,1,512]{2,1,0:T(1,128)}, f32[16,1,512]{2,1,0:T(1,128)}, u32[]{:S(2)}, u32[]{:S(2)}) collective-permute-start(f32[16,1,512]{2,1,0:T(1,128)} %get-tuple-element.12), channel_id=1, source_target_pairs={{0,1},{1,2},{2,3},{3,4},{4,5},{5,6},{6,7},{7,8},{8,9},{9,10},{10,1... | collective-permute-start | bytes 98312 | tf_op jit(solution)/shard_map/ppermute | solution.py:18
  100.3 22.7 %collective-permute-start.15 = (f32[16,1,512]{2,1,0:T(1,128)}, f32[16,1,512]{2,1,0:T(1,128)}, u32[]{:S(2)}, u32[]{:S(2)}) collective-permute-start(f32[16,1,512]{2,1,0:T(1,128)} %get-tuple-element.13), channel_id=1, source_target_pairs={{1,0},{2,1},{3,2},{4,3},{5,4},{6,5},{7,6},{8,7},{9,8},{10,9},{11,1... | collective-permute-start | bytes 98312 | tf_op jit(solution)/shard_map/ppermute | solution.py:19
  106.6 17.2 %copy-start.2 = (f32[16,64,512]{2,1,0:T(8,128)S(1)}, f32[16,64,512]{2,1,0:T(8,128)}, u32[]{:S(2)}) copy-start(f32[16,64,512]{2,1,0:T(8,128)} %copy-done.1) | copy-start | bytes 6291460
  108.1 31.5 %all-to-all-start = ((f32[16,1,8192]{2,1,0:T(1,128)}), f32[16,1,8192]{2,1,0:T(1,128)}, u32[]{:S(2)}, u32[]{:S(2)}) async-start(f32[16,1,8192]{2,1,0:T(1,128)} %reshape.107), calls=%async_computation | async-start | bytes 1048576 | tf_op jit(solution)/shard_map/all_to_all | solution.py:74
  139.6 24.5 %all-to-all-start.1 = ((f32[16,1,8192]{2,1,0:T(1,128)}), f32[16,1,8192]{2,1,0:T(1,128)S(1)}, u32[]{:S(2)}, u32[]{:S(2)}) async-start(f32[16,1,8192]{2,1,0:T(1,128)} %reshape.109), calls=%async_computation.1 | async-start | bytes 1048576 | tf_op jit(solution)/shard_map/all_to_all | solution.py:74
  150.6 15.8 %copy-start.6 = (s32[16]{0:T(128)S(1)}, s32[16]{0:T(128)}, u32[]{:S(2)}) copy-start(s32[16]{0:T(128)} %param.7) | copy-start | bytes 196
  (4 other events, 6.8 us)
